TPU v7x, 32 devices: a whole 2x2x4 slice. The times are simulated.
32 devices in a mesh: groups: 2 (over y), dp: 4 (over x, core), tensor: 4 (over z).
Axes of the slice: x: 2, y: 2, z: 4, core: 2. Of those that a mesh axis runs over, the one named last changes fastest.
Arguments:
- hidden_in: bfloat16 [256, 8192], P(('groups', 'tensor'), 'dp'), parts along dimension 0, may hold values from -45 to 45
- gain: float32 [8192], P('dp'), may hold values from 0.25 to 1.75
- w_gate: bfloat16 [8192, 14336], P('dp', 'tensor'), may hold values from -0.0625 to 0.0625
- w_up: bfloat16 [8192, 14336], P('dp', 'tensor'), may hold values from -0.0625 to 0.0625
- w_down: bfloat16 [14336, 8192], P('tensor', 'dp'), may hold values from -0.046875 to 0.046875
- exit_layer: int32 [256], P(('groups', 'tensor')), parts along dimension 0, may hold values from 1 to 80, as said below
Outputs:
- mixed: bfloat16 [256, 8192], P(('groups', 'tensor'), 'dp'), parts along dimension 0
There are 2 independent parts, one for each index of `groups`. A program takes and returns all parts, laid end to end along the dimension named above; an argument that names none is the same for every part. Nothing has to cross between parts.
Inputs may be any that keep to these rules, and one draw needn't show every extreme that they name: In each aligned block of 32 rows (the rows of one index of tensor) at most 16 rows have exit_layer above 40; some block has exactly 16, and all blocks of a part may have exactly 16.
All inputs are finite; a program needn't handle non-finite values.
Results may differ from a plain program's by a relative error of at most 0.0055.
Values may be sent and summed in bfloat16 or wider, within the bound.
A program may use at most 128 MiB of HBM per device.

v0:
```python
import jax
import jax.numpy as jnp
from jax import lax
from jax.sharding import PartitionSpec as P

D = 8192
LAYER = 40
SURV_MAX = 16


EPS = 1e-05


def local(hidden_in, gain, w_gate, w_up, w_down, exit_layer):
    kept_mask = exit_layer > LAYER
    slot_rank = jnp.cumsum(kept_mask.astype(jnp.int32)) - 1
    slot_ids = jnp.arange(SURV_MAX, dtype=jnp.int32)
    selector = ((slot_rank[None, :] == slot_ids[:, None]) & kept_mask[None, :]).astype(jnp.bfloat16)
    outgoing = jnp.dot(selector, hidden_in, preferred_element_type=jnp.float32).astype(jnp.bfloat16)
    rows_all = lax.all_gather(outgoing, "tensor", axis=0, tiled=True)
    square_part = jnp.sum(jnp.square(rows_all.astype(jnp.float32)), axis=1)
    scaled = (rows_all.astype(jnp.float32) * gain).astype(jnp.bfloat16)
    gate_part = jnp.dot(scaled, w_gate, preferred_element_type=jnp.float32).astype(jnp.bfloat16)
    up_part = jnp.dot(scaled, w_up, preferred_element_type=jnp.float32).astype(jnp.bfloat16)
    gate, up = (
        lax.psum_scatter(gate_part, "dp", scatter_dimension=0, tiled=True).astype(jnp.float32),
        lax.psum_scatter(up_part, "dp", scatter_dimension=0, tiled=True).astype(jnp.float32),
    )
    square_sum = lax.psum_scatter(square_part, "dp", scatter_dimension=0, tiled=True)
    inv_rms = lax.rsqrt(square_sum / D + EPS)
    act_share = (jax.nn.silu(gate * inv_rms[:, None]) * (up * inv_rms[:, None])).astype(
        jnp.bfloat16
    )
    activated = lax.all_gather(act_share, "dp", axis=0, tiled=True)
    own_term = lax.psum_scatter(
        jnp.dot(activated, w_down, preferred_element_type=jnp.float32).astype(jnp.bfloat16),
        "tensor",
        scatter_dimension=0,
        tiled=True,
    ).astype(jnp.float32)
    slot_rank = jnp.cumsum(kept_mask.astype(jnp.int32)) - 1
    clipped = jnp.clip(slot_rank, 0, SURV_MAX - 1)
    branch = jnp.take(own_term, clipped, axis=0)
    values = hidden_in.astype(jnp.float32)
    mixed = values + jnp.where(kept_mask[:, None], branch, jnp.float32(0.0))
    return mixed.astype(jnp.bfloat16)


def solution(mesh):
    placed = (
        P(("groups", "tensor"), "dp"),
        P("dp"),
        P("dp", "tensor"),
        P("dp", "tensor"),
        P("tensor", "dp"),
        P(("groups", "tensor")),
    )
    return jax.shard_map(
        local, mesh=mesh, in_specs=placed, out_specs=P(("groups", "tensor"), "dp"), check_vma=False
    )
```

profile of v0, /device:TPU:0, one launch (start us, length us, event | category | flops | bytes accessed | tf_op | source)
XLA Modules:
  0.0 124.5 jit_solution(3885750124560220488)
XLA Ops:
  6.5 0.0 copy-start.1
  6.5 0.0 reduce-scatter.6.cloned.1.call-start
  6.5 0.7 broadcast_compare_fusion
  7.2 0.1 copy.9
  7.3 0.1 reduce-window.4
  7.4 0.1 fusion.4
  7.5 1.0 convolution_convert_fusion.3
  8.5 15.6 %all_gather.6 = bf16[64,2048]{1,0:T(8,128)(2,1)S(1)} all-gather(bf16[16,2048]{1,0:T(8,128)(2,1)S(1)} %convolution_convert_fusion.3), channel_id=1, replica_groups=mesh['groups'=2,'dp'=4,'tensor'=4] {'tensor'}, dimensions={0}, use_global_device_ids=true | all-gather | bytes 327680 | tf_op jit(solution)/shard_map/all_gather | solution.py:20
  24.1 8.6 %convolution_convert_fusion = bf16[64,3584]{1,0:T(8,128)(2,1)} fusion(bf16[2048,3584]{1,0:T(8,128)(2,1)} %param.9, bf16[64,2048]{1,0:T(8,128)(2,1)S(1)} %all_gather.6, f32[2048]{0:T(1024)} %param.7), kind=kOutput, calls=%fused_computation.1 | convolution fusion | flops 940146688 | bytes 15409152 | tf_op jit(solution)/shard_map/dot_general | solution.py:24
  32.7 0.0 copy-start.2
  32.7 0.0 reduce-scatter.6.cloned.1.call-update
  32.8 0.0 reduce-scatter.4.cloned.1.call-start
  32.8 0.0 copy-done.1
  32.8 8.6 %convolution_convert_fusion.1 = bf16[64,3584]{1,0:T(8,128)(2,1)} fusion(bf16[2048,3584]{1,0:T(8,128)(2,1)} %param.8, bf16[64,2048]{1,0:T(8,128)(2,1)S(1)} %all_gather.6, f32[2048]{0:T(1024)S(1)} %copy-done.1), kind=kOutput, calls=%fused_computation.2 | convolution fusion | flops 940146688 | bytes 15409152 | tf_op jit(solution)/shard_map/dot_general | solution.py:23
  41.4 0.0 copy-start
  41.4 0.0 reduce-scatter.4.cloned.1.call-update
  41.4 0.0 reduce-scatter.8.cloned.1.call-start
  41.5 0.0 copy-done.2
  41.5 0.6 dynamic-slice
  42.7 0.2 fusion.1
  42.9 5.7 %all-reduce = f32[64]{0:T(128)S(1)} all-reduce(f32[64]{0:T(128)S(1)} %fusion.1), channel_id=3, replica_groups=mesh['groups'=2,'dp'=4,'tensor'=4] {'dp'}, use_global_device_ids=true, to_apply=%region_3.4.clone | all-reduce | flops 64 | bytes 512
  48.5 0.1 fusion.10
  48.6 7.0 %reduce-scatter.6.cloned.1.call-done = bf16[16,3584]{1,0:T(8,128)(2,1)} async-done(((bf16[64,3584]{1,0:T(8,128)(2,1)}), bf16[16,3584]{1,0:T(8,128)(2,1)}) %reduce-scatter.6.cloned.1.call-update) | async-done | bytes 114704 | tf_op jit(solution)/shard_map/reduce_scatter | solution.py:27
  55.7 23.8 %reduce-scatter.4.cloned.1.call-done = bf16[16,3584]{1,0:T(8,128)(2,1)} async-done(((bf16[64,3584]{1,0:T(8,128)(2,1)}), bf16[16,3584]{1,0:T(8,128)(2,1)}) %reduce-scatter.4.cloned.1.call-update) | async-done | bytes 114704 | tf_op jit(solution)/shard_map/reduce_scatter | solution.py:26
  79.4 1.1 multiply_convert_fusion
  80.5 6.4 %all_gather.7 = bf16[64,3584]{1,0:T(8,128)(2,1)S(1)} all-gather(bf16[16,3584]{1,0:T(8,128)(2,1)S(1)} %multiply_convert_fusion), channel_id=1, replica_groups=mesh['groups'=2,'dp'=4,'tensor'=4] {'dp'}, dimensions={0}, use_global_device_ids=true | all-gather | bytes 573440 | tf_op jit(solution)/shard_map/all_gather | solution.py:34
  87.0 8.6 %convolution_convert_fusion.2 = bf16[64,2048]{1,0:T(8,128)(2,1)} fusion(bf16[64,3584]{1,0:T(8,128)(2,1)S(1)} %all_gather.7, bf16[3584,2048]{1,0:T(8,128)(2,1)} %param.10), kind=kOutput, calls=%fused_computation.3 | convolution fusion | flops 939655168 | bytes 15400960 | tf_op jit(solution)/shard_map/dot_general | solution.py:36
  95.6 0.0 reduce-scatter.8.cloned.1.call-update
  95.6 20.0 %reduce-scatter.8.cloned.1.call-done = bf16[16,2048]{1,0:T(8,128)(2,1)} async-done(((bf16[64,2048]{1,0:T(8,128)(2,1)}), bf16[16,2048]{1,0:T(8,128)(2,1)}) %reduce-scatter.8.cloned.1.call-update) | async-done | bytes 65552 | tf_op jit(solution)/shard_map/reduce_scatter | solution.py:35
  115.7 0.8 convert_element_type.50
  116.5 0.7 gather_fusion
  117.2 0.0 copy-done
  117.2 0.8 add_convert_fusion
  (2 shorter events, 0.0 us)
Async XLA Ops:
  6.5 26.3 %copy-start.1 = (f32[2048]{0:T(1024)S(1)}, f32[2048]{0:T(1024)}, u32[]{:S(2)}) copy-start(f32[2048]{0:T(1024)} %param.7) | copy-start | bytes 24580
  6.5 49.1 %reduce-scatter.6.cloned.1.call-start = ((), (), s32[]{:S(2)}) async-start(), calls=%async_computation.4 | async-start | bytes 573440 | tf_op jit(solution)/shard_map/reduce_scatter | solution.py:27
  32.7 8.7 %copy-start.2 = (u32[32]{0:T(128)S(1)}, u32[32]{0:T(128)}, u32[]{:S(2)}) copy-start(u32[32]{0:T(128)} %constant.39) | copy-start | bytes 388
  32.8 46.7 %reduce-scatter.4.cloned.1.call-start = ((), (), s32[]{:S(2)}) async-start(), calls=%async_computation.3 | async-start | bytes 573440 | tf_op jit(solution)/shard_map/reduce_scatter | solution.py:26
  41.4 75.8 %copy-start = (bf16[32,2048]{1,0:T(8,128)(2,1)S(1)}, bf16[32,2048]{1,0:T(8,128)(2,1)}, u32[]{:S(2)}) copy-start(bf16[32,2048]{1,0:T(8,128)(2,1)} %param.6) | copy-start | bytes 393220
  41.4 74.3 %reduce-scatter.8.cloned.1.call-start = ((), (), s32[]{:S(2)}) async-start(), calls=%async_computation.5 | async-start | bytes 327680 | tf_op jit(solution)/shard_map/reduce_scatter | solution.py:35
Sparse Core Ops, SparseCore 0:
  32.9 22.7 reduce-scatter.5
  58.2 21.1 reduce-scatter.3
  95.7 19.9 reduce-scatter.7
where the time goes:
time: 125 us; the launch traced here: 124 us
  waiting for transfers between devices  50.9 us (41%)
  blocking collectives  27.7 us (22%)
  matrix products  26.8 us (21%)
  between operations  13.8 us (11%)
  other arithmetic  3.82 us (3%)
  local copies, waits for them, and re-layouts  1.34 us (1%)
    reduce_scatter x1, waiting for transfers between devices, local(): lax.psum_scatter(gate_part, 'dp', scatter_dimension=0, tiled=True)  23.8 us
    reduce_scatter x1, waiting for transfers between devices, local(): lax.psum_scatter(jnp.dot(activated, w_down, preferred_element_type=jnp.fl...  20 us
    all_gather x1, blocking collectives, local(): rows_all = lax.all_gather(outgoing, 'tensor', axis=0, tiled=True)  15.6 us
    dot_general x1, matrix products, local(): jnp.dot(activated, w_down, preferred_element_type=jnp.float32)  8.6 us
    dot_general x1, matrix products, local(): jnp.dot(scaled, w_up, preferred_element_type=jnp.float32)  8.58 us
    dot_general x1, matrix products, local(): jnp.dot(scaled, w_gate, preferred_element_type=jnp.float32)  8.57 us
    reduce_scatter x1, waiting for transfers between devices, local(): lax.psum_scatter(up_part, 'dp', scatter_dimension=0, tiled=True)  7.05 us
    all_gather x1, blocking collectives, local(): activated = lax.all_gather(act_share, 'dp', axis=0, tiled=True)  6.43 us
  transfers between devices with their start and end apart: 3, of which 3 were waited for; matrix products, arithmetic and copies ran while one was open for 8% of the time, Pallas kernels for 0%

commit v1 on v0

v1 whole, which is shorter than its diff:
```python
import functools

import jax
import jax.numpy as jnp
from jax import lax
from jax.experimental import pallas as pl
from jax.experimental.pallas import tpu as pltpu
from jax.sharding import PartitionSpec as P

D = 8192
LAYER = 40
SURV_MAX = 16
EPS = 1e-05
MESH = pl.DeviceIdType.MESH
F32 = jnp.float32
BF16 = jnp.bfloat16


def kernel(
    n_dp, n_t, nj, hid, gain, exits, w_gate, w_up, w_down, out,
    hid_v, gain_v, exit_v, wg_v, wu_v, wd_v,
    rows_v, xs, sq, sq_in, inv_v, sel_v,
    part, core_in, chip_sum, chip_in, act_v, acc, z_out, z_in,
    in_sem, wg_sem, wu_sem, wd_sem, ag_s, ag_r, sq_s, sq_r,
    a_s, a_r, b_s, b_r, c_s, c_r, p_s, p_r, f_s, f_r, z_s, z_r,
):
    n_x = n_dp // 2
    me_dp = lax.axis_index("dp")
    me_t = lax.axis_index("tensor")
    x = me_dp // 2
    c = me_dp % 2
    other = x * 2 + (1 - c)
    slots, d_l = SURV_MAX, hid.shape[1]
    tok = hid.shape[0]
    n_rows = n_t * slots
    half = n_rows // 2
    blk = n_rows // n_dp
    width = wg_v.shape[2]

    def remote(src, dst, send, recv, **where):
        return pltpu.make_async_remote_copy(
            src_ref=src, dst_ref=dst, send_sem=send, recv_sem=recv,
            device_id=where, device_id_type=MESH,
        )

    barrier = pltpu.get_barrier_semaphore()
    for o in range(1, n_t):
        pl.semaphore_signal(barrier, inc=1, device_id={"tensor": (me_t + o) % n_t}, device_id_type=MESH)
    for o in range(1, n_dp):
        pl.semaphore_signal(barrier, inc=1, device_id={"dp": (me_dp + o) % n_dp}, device_id_type=MESH)

    small = [
        pltpu.make_async_copy(hid, hid_v, in_sem.at[0]),
        pltpu.make_async_copy(exits, exit_v, in_sem.at[1]),
        pltpu.make_async_copy(gain, gain_v, in_sem.at[2]),
    ]
    for cp in small:
        cp.start()

    def col(j):
        return pl.ds(pl.multiple_of(j * width, width), width) if nj > 1 else pl.ds(0, width)

    def gate_copy(j):
        return pltpu.make_async_copy(w_gate.at[:, col(j)], wg_v.at[j], wg_sem.at[j])

    def up_copy(j):
        return pltpu.make_async_copy(w_up.at[:, col(j)], wu_v.at[j], wu_sem.at[j])

    def down_copy(j):
        return pltpu.make_async_copy(w_down.at[col(j), :], wd_v.at[j], wd_sem.at[j])

    @pl.loop(0, nj)
    def _(j):
        gate_copy(j).start()
        up_copy(j).start()

    for cp in small:
        cp.wait()

    kept = exit_v[...] > LAYER
    r_id = lax.broadcasted_iota(jnp.int32, (tok, tok), 0)
    c_id = lax.broadcasted_iota(jnp.int32, (tok, tok), 1)
    tri = (r_id <= c_id).astype(F32)
    rank = jnp.dot(kept.astype(F32), tri, preferred_element_type=F32) - 1.0
    s_id = lax.broadcasted_iota(jnp.int32, (slots, tok), 0).astype(F32)
    kept_b = jnp.broadcast_to(kept.astype(F32), (slots, tok))
    sel = jnp.where(jnp.broadcast_to(rank, (slots, tok)) == s_id, kept_b, 0.0)
    sel_v[...] = sel
    rows_v[me_t] = jnp.dot(sel.astype(BF16), hid_v[...], preferred_element_type=F32).astype(BF16)

    pl.semaphore_wait(barrier, n_t + n_dp - 2)

    def ag_copy(o, src):
        return remote(rows_v.at[src], rows_v.at[src], ag_s.at[o - 1], ag_r.at[o - 1], tensor=(me_t + o) % n_t)

    for o in range(1, n_t):
        ag_copy(o, me_t).start()

    def take_rows(t):
        v = rows_v[t].astype(F32)
        xs[t] = (v * gain_v[...]).astype(BF16)
        total = v[:, :128] * v[:, :128]
        for k in range(1, d_l // 128):
            piece = v[:, k * 128:(k + 1) * 128]
            total = total + piece * piece
        sq[pl.ds(pl.multiple_of(t * slots, slots), slots), :] = total

    take_rows(me_t)
    for o in range(1, n_t):
        src = (me_t + n_t - o) % n_t
        ag_copy(o, src).wait_recv()
        take_rows(src)

    def place(d):
        return (d % 2) * n_x + d // 2

    def rows_of(b):
        return pl.ds(pl.multiple_of(b * blk, blk), blk)

    def sq_copy(o):
        d = (me_dp + o) % n_dp
        return remote(sq.at[rows_of(place(d)), :], sq_in.at[o - 1], sq_s.at[o - 1], sq_r.at[o - 1], dp=d)

    for o in range(1, n_dp):
        sq_copy(o).start()

    acc[...] = jnp.zeros_like(acc)

    mine = c * n_x + x
    lead = max(nj, 4)

    def a_copy(j):
        return remote(part.at[j, 1 - c], core_in.at[j], a_s.at[j], a_r.at[j], dp=other)

    def b_copy(j, o):
        xd = (x + o) % n_x
        return remote(chip_sum.at[j, xd], chip_in.at[j, o - 1], b_s.at[j, o - 1], b_r.at[j, o - 1], dp=xd * 2 + c)

    def c_copy(j, o, b):
        xd = (x + o) % n_x
        return remote(act_v.at[j, b], act_v.at[j, b], c_s.at[j, o - 1], c_r.at[j, o - 1], dp=xd * 2 + c)

    def p_copy(j, b):
        return remote(act_v.at[j, b], act_v.at[j, b], p_s.at[j], p_r.at[j], dp=other)

    def f_copy(j, o, b):
        return remote(act_v.at[j, b], act_v.at[j, b], f_s.at[j, o - 1], f_r.at[j, o - 1], dp=other)

    @pl.loop(0, nj + lead)
    def _(it):
        @pl.when(it < nj)
        def _():
            j = it
            down_copy(j).start()
            xv = xs[...].reshape(n_rows, d_l)
            for m, (copy, w) in enumerate(((gate_copy, wg_v), (up_copy, wu_v))):
                copy(j).wait()
                p = jnp.dot(xv, w[j], preferred_element_type=F32).astype(BF16)
                part[j, 0, m] = p[:half]
                part[j, 1, m] = p[half:]
            a_copy(j).start()

        @pl.when((it >= 1) & (it < nj + 1))
        def _():
            j = it - 1
            a_copy(j).wait_recv()
            s = part[j, c].astype(F32) + core_in[j].astype(F32)
            for b in range(n_x):
                chip_sum[j, b] = s[:, b * blk:(b + 1) * blk].astype(BF16)
            for o in range(1, n_x):
                b_copy(j, o).start()

        @pl.when(it == 2)
        def _():
            total = sq[rows_of(mine), :]
            for o in range(1, n_dp):
                sq_copy(o).wait_recv()
                total = total + sq_in[o - 1]
            ms = jnp.sum(total, axis=1, keepdims=True) / D
            inv_v[...] = jnp.broadcast_to(lax.rsqrt(ms + EPS), inv_v.shape)

        @pl.when((it >= 2) & (it < nj + 2))
        def _():
            j = it - 2
            t = part[j, c, :, rows_of(x), :].astype(F32) + core_in[j, :, rows_of(x), :].astype(F32)
            for o in range(1, n_x):
                b_copy(j, o).wait_recv()
                t = t + chip_in[j, o - 1].astype(F32)
            inv = inv_v[:, :1]
            g = t[0] * inv
            u = t[1] * inv
            act_v[j, mine] = (g / (1.0 + jnp.exp(-g)) * u).astype(BF16)
            for o in range(1, n_x):
                c_copy(j, o, mine).start()
            p_copy(j, mine).start()

        @pl.when((it >= 3) & (it < nj + 3))
        def _():
            j = it - 3
            for o in range(1, n_x):
                b = c * n_x + (x + n_x - o) % n_x
                c_copy(j, o, b).wait_recv()
                f_copy(j, o, b).start()

        @pl.when(it >= lead)
        def _():
            j = it - lead
            p_copy(j, (1 - c) * n_x + x).wait_recv()
            for o in range(1, n_x):
                f_copy(j, o, (1 - c) * n_x + (x + n_x - o) % n_x).wait_recv()
            down_copy(j).wait()
            a = act_v[j].reshape(n_rows, width)
            acc[...] += jnp.dot(a, wd_v[j], preferred_element_type=F32)

    def z_copy(o):
        t = (me_t + o) % n_t
        return remote(z_out.at[t], z_in.at[o - 1], z_s.at[o - 1], z_r.at[o - 1], tensor=t)

    for o in range(1, n_t):
        t = (me_t + o) % n_t
        z_out[t] = acc[pl.ds(pl.multiple_of(t * slots, slots), slots), :].astype(BF16)
        z_copy(o).start()
    total = acc[pl.ds(pl.multiple_of(me_t * slots, slots), slots), :].astype(BF16).astype(F32)

    @pl.loop(0, nj)
    def _(j):
        a_copy(j).wait_send()
        p_copy(j, mine).wait_send()
        for o in range(1, n_x):
            b_copy(j, o).wait_send()
            c_copy(j, o, mine).wait_send()
            f_copy(j, o, c * n_x + (x + n_x - o) % n_x).wait_send()

    for o in range(1, n_t):
        ag_copy(o, me_t).wait_send()
    for o in range(1, n_dp):
        sq_copy(o).wait_send()

    for o in range(1, n_t):
        z_copy(o).wait_recv()
        total = total + z_in[o - 1].astype(F32)
    for o in range(1, n_t):
        z_copy(o).wait_send()

    sel_b = sel_v[...].astype(BF16)
    back = (((0,), (0,)), ((), ()))
    high = total.astype(BF16)
    low = (total - high.astype(F32)).astype(BF16)
    branch = lax.dot_general(sel_b, high, back, preferred_element_type=F32)
    branch = branch + lax.dot_general(sel_b, low, back, preferred_element_type=F32)
    out[...] = (hid_v[...].astype(F32) + branch).astype(BF16)


def solution(mesh):
    n_dp, n_t = mesh.shape["dp"], mesh.shape["tensor"]
    n_x = n_dp // 2

    def local(hidden_in, gain, w_gate, w_up, w_down, exit_layer):
        tok, d_l = hidden_in.shape
        f_l = w_gate.shape[1]
        width = 512 if f_l % 512 == 0 else f_l
        nj = f_l // width
        n_rows = n_t * SURV_MAX
        half, blk = n_rows // 2, n_rows // n_dp
        nx1 = max(n_x - 1, 1)
        any_spec = pl.BlockSpec(memory_space=pl.ANY)
        dma = pltpu.SemaphoreType.DMA
        vmem = pltpu.VMEM
        return pl.pallas_call(
            functools.partial(kernel, n_dp, n_t, nj),
            out_shape=jax.ShapeDtypeStruct((tok, d_l), BF16),
            in_specs=[any_spec] * 6,
            out_specs=pl.BlockSpec(memory_space=pltpu.VMEM),
            scratch_shapes=[
                vmem((tok, d_l), BF16),
                vmem((1, d_l), F32),
                vmem((1, tok), jnp.int32),
                vmem((nj, d_l, width), BF16),
                vmem((nj, d_l, width), BF16),
                vmem((nj, width, d_l), BF16),
                vmem((n_t, SURV_MAX, d_l), BF16),
                vmem((n_t, SURV_MAX, d_l), BF16),
                vmem((n_rows, 128), F32),
                vmem((n_dp - 1, blk, 128), F32),
                vmem((blk, 128), F32),
                vmem((SURV_MAX, tok), F32),
                vmem((nj, 2, 2, half, width), BF16),
                vmem((nj, 2, half, width), BF16),
                vmem((nj, n_x, 2, blk, width), BF16),
                vmem((nj, nx1, 2, blk, width), BF16),
                vmem((nj, n_dp, blk, width), BF16),
                vmem((n_rows, d_l), F32),
                vmem((n_t, SURV_MAX, d_l), BF16),
                vmem((n_t - 1, SURV_MAX, d_l), BF16),
                dma((3,)), dma((nj,)), dma((nj,)), dma((nj,)),
                dma((n_t - 1,)), dma((n_t - 1,)), dma((n_dp - 1,)), dma((n_dp - 1,)),
                dma((nj,)), dma((nj,)), dma((nj, nx1)), dma((nj, nx1)),
                dma((nj, nx1)), dma((nj, nx1)), dma((nj,)), dma((nj,)),
                dma((nj, nx1)), dma((nj, nx1)), dma((n_t - 1,)), dma((n_t - 1,)),
            ],
            compiler_params=pltpu.CompilerParams(
                collective_id=0, has_side_effects=True, vmem_limit_bytes=60 * 1024 * 1024
            ),
            name="ffn_block",
        )(hidden_in, gain.reshape(1, -1), exit_layer.reshape(1, -1), w_gate, w_up, w_down)

    placed = (
        P(("groups", "tensor"), "dp"),
        P("dp"),
        P("dp", "tensor"),
        P("dp", "tensor"),
        P("tensor", "dp"),
        P(("groups", "tensor")),
    )
    return jax.shard_map(
        local, mesh=mesh, in_specs=placed, out_specs=P(("groups", "tensor"), "dp"), check_vma=False
    )
```

time: 125 us -> 43.5 us (0.35)
  waiting for transfers between devices: 50.9 us -> 0 us
  Pallas kernels: 0 us -> 41.7 us
  blocking collectives: 27.7 us -> 0 us
  matrix products: 26.8 us -> 0 us
  between operations: 13.8 us -> 0.01 us
  other arithmetic: 3.82 us -> 0 us
    reduce_scatter x3 -> x0, waiting for transfers between devices: 50.9 us -> none  [the longest x1 23.8 us: local(): lax.psum_scatter(gate_part, 'dp', scatter_dimension=0, tiled=True)]
    pallas_call x0 -> x1, Pallas kernels: none -> 41.7 us  [local(): pl.pallas_call(functools.partial(kernel, n_dp, n_t, nj), out_shape=jax.Sh...]
    dot_general x4 -> x0, matrix products: 26.8 us -> none  [the longest x1 8.6 us: local(): jnp.dot(activated, w_down, preferred_element_type=jnp.float32)]
    all_gather x2 -> x0, blocking collectives: 22.1 us -> none  [the longest x1 15.6 us: local(): rows_all = lax.all_gather(outgoing, 'tensor', axis=0, tiled=True)]
    unnamed x1 -> x0, blocking collectives: 5.66 us -> none
    convert_element_type x3 -> x0, other arithmetic: 2.72 us -> none  [the longest x1 1.11 us: local(): (jax.nn.silu(gate * inv_rms[:, None]) * (up * inv_rms[:, None])).astype(j...]
  transfers between devices with their start and end apart: 3 -> 0, of which waited for: 3 -> 0; matrix products, arithmetic and copies ran while one was open for 8% -> 0% of each run, Pallas kernels for 0% -> 0%
where the time goes in v1:
time: 43.5 us; the launch traced here: 43.3 us
  Pallas kernels  41.7 us (96%)
  local copies, waits for them, and re-layouts  1.57 us (4%)
    pallas_call x1, Pallas kernels, local(): pl.pallas_call(functools.partial(kernel, n_dp, n_t, nj), out_shape=jax.Sh...  41.7 us
    unnamed x1, local copies, waits for them, and re-layouts  1.57 us

profile of v1, /device:TPU:0, one launch (start us, length us, event | category | flops | bytes accessed | tf_op | source)
XLA Modules:
  0.0 43.3 jit_solution(16342864192955566352)
XLA Ops:
  0.0 41.7 %ffn_block.1 = bf16[32,2048]{1,0:T(8,128)(2,1)} custom-call(bf16[32,2048]{1,0:T(8,128)(2,1)} %hid.1, f32[1,2048]{1,0:T(1,128)} %bitcast.2, s32[1,32]{1,0:T(1,128)} %bitcast.3, bf16[2048,3584]{1,0:T(8,128)(2,1)} %w_gate.1, bf16[2048,3584]{1,0:T(8,128)(2,1)} %w_up.1, bf16[3584,2048]{1,0:T(8,128)(2,1)} %w_down.1), custom_call_target="tpu_custom_call" | custom-call | tf_op jit(solution)/shard_map/ffn_block/pallas_call | solution.py:269
  41.7 1.6 %copy.8 = bf16[32,2048]{1,0:T(8,128)(2,1)} copy(bf16[32,2048]{1,0:T(8,128)(2,1)} %ffn_block.1) | data formatting | bytes 262144

commit v2 on v1

--- a/solution.py
+++ b/solution.py
@@ -11,6 +11,7 @@
 LAYER = 40
 SURV_MAX = 16
 EPS = 1e-05
+LAG = 2
 MESH = pl.DeviceIdType.MESH
 F32 = jnp.float32
 BF16 = jnp.bfloat16
@@ -127,7 +128,7 @@
     acc[...] = jnp.zeros_like(acc)
 
     mine = c * n_x + x
-    lead = max(nj, 4)
+    lead = max(nj, 2 * LAG + 1)
 
     def a_copy(j):
         return remote(part.at[j, 1 - c], core_in.at[j], a_s.at[j], a_r.at[j], dp=other)
@@ -144,7 +145,8 @@
         return remote(act_v.at[j, b], act_v.at[j, b], p_s.at[j], p_r.at[j], dp=other)
 
     def f_copy(j, o, b):
-        return remote(act_v.at[j, b], act_v.at[j, b], f_s.at[j, o - 1], f_r.at[j, o - 1], dp=other)
+        xd = (x + o) % n_x
+        return remote(act_v.at[j, b], act_v.at[j, b], f_s.at[j, o - 1], f_r.at[j, o - 1], dp=xd * 2 + 1 - c)
 
     @pl.loop(0, nj + lead)
     def _(it):
@@ -160,9 +162,21 @@
                 part[j, 1, m] = p[half:]
             a_copy(j).start()
 
-        @pl.when((it >= 1) & (it < nj + 1))
-        def _():
-            j = it - 1
+        @pl.when(it >= lead)
+        def _():
+            j = it - lead
+            p_copy(j, (1 - c) * n_x + x).wait_recv()
+            for o in range(1, n_x):
+                xs_o = (x + n_x - o) % n_x
+                c_copy(j, o, c * n_x + xs_o).wait_recv()
+                f_copy(j, o, (1 - c) * n_x + xs_o).wait_recv()
+            down_copy(j).wait()
+            a = act_v[j].reshape(n_rows, width)
+            acc[...] += jnp.dot(a, wd_v[j], preferred_element_type=F32)
+
+        @pl.when((it >= LAG) & (it < nj + LAG))
+        def _():
+            j = it - LAG
             a_copy(j).wait_recv()
             s = part[j, c].astype(F32) + core_in[j].astype(F32)
             for b in range(n_x):
@@ -170,7 +184,7 @@
             for o in range(1, n_x):
                 b_copy(j, o).start()
 
-        @pl.when(it == 2)
+        @pl.when(it == 2 * LAG)
         def _():
             total = sq[rows_of(mine), :]
             for o in range(1, n_dp):
@@ -179,9 +193,9 @@
             ms = jnp.sum(total, axis=1, keepdims=True) / D
             inv_v[...] = jnp.broadcast_to(lax.rsqrt(ms + EPS), inv_v.shape)
 
-        @pl.when((it >= 2) & (it < nj + 2))
-        def _():
-            j = it - 2
+        @pl.when((it >= 2 * LAG) & (it < nj + 2 * LAG))
+        def _():
+            j = it - 2 * LAG
             t = part[j, c, :, rows_of(x), :].astype(F32) + core_in[j, :, rows_of(x), :].astype(F32)
             for o in range(1, n_x):
                 b_copy(j, o).wait_recv()
@@ -192,25 +206,8 @@
             act_v[j, mine] = (g / (1.0 + jnp.exp(-g)) * u).astype(BF16)
             for o in range(1, n_x):
                 c_copy(j, o, mine).start()
+                f_copy(j, o, mine).start()
             p_copy(j, mine).start()
-
-        @pl.when((it >= 3) & (it < nj + 3))
-        def _():
-            j = it - 3
-            for o in range(1, n_x):
-                b = c * n_x + (x + n_x - o) % n_x
-                c_copy(j, o, b).wait_recv()
-                f_copy(j, o, b).start()
-
-        @pl.when(it >= lead)
-        def _():
-            j = it - lead
-            p_copy(j, (1 - c) * n_x + x).wait_recv()
-            for o in range(1, n_x):
-                f_copy(j, o, (1 - c) * n_x + (x + n_x - o) % n_x).wait_recv()
-            down_copy(j).wait()
-            a = act_v[j].reshape(n_rows, width)
-            acc[...] += jnp.dot(a, wd_v[j], preferred_element_type=F32)
 
     def z_copy(o):
         t = (me_t + o) % n_t
@@ -229,7 +226,7 @@
         for o in range(1, n_x):
             b_copy(j, o).wait_send()
             c_copy(j, o, mine).wait_send()
-            f_copy(j, o, c * n_x + (x + n_x - o) % n_x).wait_send()
+            f_copy(j, o, mine).wait_send()
 
     for o in range(1, n_t):
         ag_copy(o, me_t).wait_send()

time: 43.5 us -> 38.9 us (0.89)
  Pallas kernels: 41.7 us -> 37.1 us
    pallas_call x1, Pallas kernels: 41.7 us -> 37.1 us  [local(): pl.pallas_call(functools.partial(kernel, n_dp, n_t, nj), out_shape=jax.Sh...]
where the time goes in v2:
time: 38.9 us; the launch traced here: 38.7 us
  Pallas kernels  37.1 us (95%)
  local copies, waits for them, and re-layouts  1.57 us (4%)
    pallas_call x1, Pallas kernels, local(): pl.pallas_call(functools.partial(kernel, n_dp, n_t, nj), out_shape=jax.Sh...  37.1 us
    unnamed x1, local copies, waits for them, and re-layouts  1.57 us

profile of v2, /device:TPU:0, one launch (start us, length us, event | category | flops | bytes accessed | tf_op | source)
XLA Modules:
  0.0 38.7 jit_solution(14361272230544489497)
XLA Ops:
  0.0 37.1 %ffn_block.1 = bf16[32,2048]{1,0:T(8,128)(2,1)} custom-call(bf16[32,2048]{1,0:T(8,128)(2,1)} %hid.1, f32[1,2048]{1,0:T(1,128)} %bitcast.2, s32[1,32]{1,0:T(1,128)} %bitcast.3, bf16[2048,3584]{1,0:T(8,128)(2,1)} %w_gate.1, bf16[2048,3584]{1,0:T(8,128)(2,1)} %w_up.1, bf16[3584,2048]{1,0:T(8,128)(2,1)} %w_down.1), custom_call_target="tpu_custom_call" | custom-call | tf_op jit(solution)/shard_map/ffn_block/pallas_call | solution.py:266
  37.2 1.6 %copy.8 = bf16[32,2048]{1,0:T(8,128)(2,1)} copy(bf16[32,2048]{1,0:T(8,128)(2,1)} %ffn_block.1) | data formatting | bytes 262144
